TPU v7x, 256 devices: a whole 4x4x8 slice. The times are simulated.
256 devices in a mesh: dp: 16 (over z, core), ulysses: 8 (over y, x_hi), tensor: 2 (over x_lo).
Axes of the slice: x: 4 (x_hi: 2, x_lo: 2; x = x_hi * 2 + x_lo), y: 4, z: 8, core: 2. Of those that a mesh axis runs over, the one named last changes fastest.
Arguments:
- queries: bfloat16 [49152, 2048], P(('dp', 'ulysses'), 'tensor'), parts along dimension 0, may hold values from -128 to 128
- key_vectors: bfloat16 [49152, 2048], P(('dp', 'ulysses'), 'tensor'), parts along dimension 0, may hold values from -6 to 6
- value_vectors: bfloat16 [49152, 2048], P(('dp', 'ulysses'), 'tensor'), parts along dimension 0, may hold values from -6 to 6
- window_tiles: int32 [128, 6], P('dp'), parts along dimension 0, may hold values from -1 to 7, as said below
- out_weight: bfloat16 [2048, 3072], P('tensor', 'ulysses'), may hold values from -0.1875 to 0.1875
Outputs:
- mixed: bfloat16 [49152, 3072], P(('dp', 'ulysses'), 'tensor'), parts along dimension 0
There are 16 independent parts, one for each index of `dp`. A program takes and returns all parts, laid end to end along the dimension named above; an argument that names none is the same for every part. Nothing has to cross between parts.
Inputs may be any that keep to these rules, and one draw needn't show every extreme that they name: `window_tiles`: tiles form a grid of 4 x 1 x 2 (time slowest; tile t*2 + h*2 + w). Row i lists, in an order drawn from the seed, tile i itself and a subset drawn from the seed of the tiles whose three grid positions each differ from tile i's by at most one, each listed at most once; the remaining slots hold -1.
All inputs are finite; a program needn't handle non-finite values.
Results may differ from a plain program's by a relative error of at most 0.0057.
Values may be sent and summed in bfloat16 or wider, within the bound.
A program may use at most 64 MiB of HBM per device.

v0:
```python
import jax
import jax.numpy as jnp
from jax import lax
from jax.sharding import PartitionSpec as P

HD = 128
TILE = 384
WMAX = 6


def grouped_attention(query_head, key_head, value_head, window_tiles):
    tile_count = query_head.shape[0] // TILE
    key_tiles = key_head.reshape(tile_count, TILE, HD)
    value_tiles = value_head.reshape(tile_count, TILE, HD)
    query_groups = query_head.reshape(tile_count // 2, 2, TILE, HD)
    window_groups = window_tiles.reshape(tile_count // 2, 2, WMAX)
    scale = HD ** (-0.5)

    def per_group(pair):
        query_pair, window_pair = pair
        valid_slot = window_pair >= 0
        safe_index = jnp.maximum(window_pair, 0)
        key_block = key_tiles[safe_index].reshape(2, WMAX * TILE, HD)
        value_block = value_tiles[safe_index].reshape(2, WMAX * TILE, HD)
        scores = (
            jnp.einsum("gqd,gkd->gqk", query_pair, key_block, preferred_element_type=jnp.float32)
            * scale
        )
        allowed = jnp.repeat(valid_slot, TILE, axis=1)[:, None, :]
        scores = jnp.where(allowed, scores, -1e30)
        peak_score = jnp.max(scores, axis=2, keepdims=True)
        exp_scores = jnp.exp(scores - peak_score)
        weights = (exp_scores / jnp.sum(exp_scores, axis=2, keepdims=True)).astype(jnp.bfloat16)
        return jnp.einsum(
            "gqk,gkd->gqd", weights, value_block, preferred_element_type=jnp.float32
        ).astype(jnp.bfloat16)

    result = lax.map(per_group, (query_groups, window_groups))
    return result.reshape(tile_count * TILE, HD)


def on_device(queries, key_vectors, value_vectors, window_tiles, out_weight):
    local_rows, local_width = queries.shape
    ulysses_size = lax.axis_size("ulysses")
    head_count = local_width // HD
    per_device = head_count // ulysses_size

    def arrange(values):
        return values.reshape(local_rows, ulysses_size, per_device, HD)

    query_all = lax.all_to_all(arrange(queries), "ulysses", split_axis=1, concat_axis=0, tiled=True)
    key_all = lax.all_to_all(
        arrange(key_vectors), "ulysses", split_axis=1, concat_axis=0, tiled=True
    )
    value_all = lax.all_to_all(
        arrange(value_vectors), "ulysses", split_axis=1, concat_axis=0, tiled=True
    )

    def heads_first(values):
        return jnp.transpose(values[:, 0], (1, 0, 2))

    def one_head(triple):
        return grouped_attention(triple[0], triple[1], triple[2], window_tiles)

    result = lax.map(
        one_head, (heads_first(query_all), heads_first(key_all), heads_first(value_all))
    )
    attention = jnp.transpose(result, (1, 0, 2))[:, None]
    returned = lax.all_to_all(attention, "ulysses", split_axis=0, concat_axis=1, tiled=True)
    attention_rows = returned.reshape(local_rows, local_width)
    partial_out = jnp.dot(
        attention_rows,
        lax.all_gather(out_weight, "ulysses", axis=1, tiled=True),
        preferred_element_type=jnp.float32,
    )
    mixed = lax.psum_scatter(partial_out, "tensor", scatter_dimension=1, tiled=True).astype(
        jnp.bfloat16
    )
    return mixed


def solution(mesh):
    in_specs = (
        P(("dp", "ulysses"), "tensor"),
        P(("dp", "ulysses"), "tensor"),
        P(("dp", "ulysses"), "tensor"),
        P("dp", None),
        P("tensor", "ulysses"),
    )
    out_specs = P(("dp", "ulysses"), "tensor")
    return jax.shard_map(
        on_device, mesh=mesh, in_specs=in_specs, out_specs=out_specs, check_vma=False
    )
```

profile of v0, /device:TPU:8, one launch (start us, length us, event | category | flops | bytes accessed | tf_op | source)
XLA Modules:
  0.0 216.9 jit_solution(12347750650175854211)
XLA Ops:
  7.3 2.3 %copy.27 = bf16[384,1024]{0,1:T(8,128)(2,1)} copy(bf16[384,1024]{1,0:T(8,128)(2,1)} %param.8) | data formatting | bytes 1572864 | tf_op args[1]
  9.5 7.4 %all-to-all-start.1 = ((bf16[384,8,1,128]{0,3,2,1:T(8,128)(2,1)}), bf16[384,8,1,128]{0,3,2,1:T(8,128)(2,1)S(1)}, u32[]{:S(2)}, u32[]{:S(2)}) async-start(bf16[384,8,1,128]{0,3,2,1:T(8,128)(2,1)} %bitcast.11), calls=%async_computation.1 | async-start | bytes 1572864 | tf_op jit(solution)/shard_map/all_to_all | solution.py:52
  18.1 10.7 %all-to-all-done.1 = bf16[384,8,1,128]{0,3,2,1:T(8,128)(2,1)S(1)} async-done(((bf16[384,8,1,128]{0,3,2,1:T(8,128)(2,1)}), bf16[384,8,1,128]{0,3,2,1:T(8,128)(2,1)S(1)}, u32[]{:S(2)}, u32[]{:S(2)}) %all-to-all-start.1) | async-done | bytes 786464 | tf_op jit(solution)/shard_map/all_to_all | solution.py:52
  28.8 6.1 %all-to-all-start.2 = ((bf16[384,8,1,128]{0,3,2,1:T(8,128)(2,1)}), bf16[384,8,1,128]{0,3,2,1:T(8,128)(2,1)S(1)}, u32[]{:S(2)}, u32[]{:S(2)}) async-start(bf16[384,8,1,128]{0,3,2,1:T(8,128)(2,1)} %bitcast.16), calls=%async_computation.2 | async-start | bytes 1572864 | tf_op jit(solution)/shard_map/all_to_all | solution.py:55
  36.4 10.2 %all-to-all-done.2 = bf16[384,8,1,128]{0,3,2,1:T(8,128)(2,1)S(1)} async-done(((bf16[384,8,1,128]{0,3,2,1:T(8,128)(2,1)}), bf16[384,8,1,128]{0,3,2,1:T(8,128)(2,1)S(1)}, u32[]{:S(2)}, u32[]{:S(2)}) %all-to-all-start.2) | async-done | bytes 786464 | tf_op jit(solution)/shard_map/all_to_all | solution.py:55
  46.6 8.4 %all-to-all-start = ((bf16[384,8,1,128]{3,0,2,1:T(8,128)(2,1)}), bf16[384,8,1,128]{3,0,2,1:T(8,128)(2,1)S(1)}, u32[]{:S(2)}, u32[]{:S(2)}) async-start(bf16[384,8,1,128]{3,0,2,1:T(8,128)(2,1)} %copy.26), calls=%async_computation | async-start | bytes 1572864 | tf_op jit(solution)/shard_map/all_to_all | solution.py:51
  55.8 8.8 %all-to-all-done = bf16[384,8,1,128]{3,0,2,1:T(8,128)(2,1)S(1)} async-done(((bf16[384,8,1,128]{3,0,2,1:T(8,128)(2,1)}), bf16[384,8,1,128]{3,0,2,1:T(8,128)(2,1)S(1)}, u32[]{:S(2)}, u32[]{:S(2)}) %all-to-all-start) | async-done | bytes 786464 | tf_op jit(solution)/shard_map/all_to_all | solution.py:51
  64.6 46.1 %while.17 = (s32[]{:T(128)}, bf16[4,2,384,128]{3,2,1,0:T(8,128)(2,1)}, s32[4,2,6]{2,1,0:T(2,128)}, bf16[4,2,384,128]{3,2,1,0:T(8,128)(2,1)S(1)}, bf16[8,384,128]...) while((s32[]{:T(128)}, bf16[4,2,384,128]{3,2,1,0:T(8,128)(2,1)}, s32[4,2,6]{2,1,0:T(2,128)}, ...), condition=%wide.region_3.4_spmd, body=%wide.region_0.3_spmd.sunk | while | flops 1374984448 | bytes 8891377 | solution.py:38
  67.0 3.0 %fusion.61 = f32[2,384]{1,0:T(2,128)} fusion(pred[2,2304]{1,0:T(4,128)(4,1)S(1)} %bitcast.90, bf16[2,2304,128]{2,1,0:T(8,128)(2,1)S(1)} %bitcast.80, bf16[4,2,384,128]{3,2,1,0:T(8,128)(2,1)S(1)} %get-tuple-element.146, s32[]{:T(128)} %get-tuple-element.136), kind=kOutput, calls=%fused_computation.33.clone.1 | convolution fusion | flops 460065024 | bytes 1388548 | tf_op jit(solution)/shard_map/while/body/eval_jaxpr/while/body/eval_jaxpr/sub | solution.py:32
  69.9 1.7 gather_fusion
  71.7 4.4 %fusion.62 = bf16[4,2,384,128]{3,2,1,0:T(8,128)(2,1)} fusion(bf16[4,2,384,128]{3,2,1,0:T(8,128)(2,1)} %get-tuple-element.137, s32[]{:T(128)} %get-tuple-element.136, bf16[2,2304,128]{2,1,0:T(8,128)(2,1)} %bitcast.82, f32[2,384]{1,0:T(2,128)} %fusion.61, pred[2,2304]{1,0:T(4,128)(4,1)S(1)} %bitcast.91, bf16[2,2304,128]{2,1,0:T(8,128)(2,1)S(1)} %bitcast.81, ...), kind=kOutput, calls=%fused_computation.13.clone.1 | convolution fusion | flops 914918400 | bytes 2765824 | tf_op jit(solution)/shard_map/while/body/eval_jaxpr/while/body/eval_jaxpr/gqk,gkd->gqd/dot_general | solution.py:34
  78.5 3.0 %fusion.61 = f32[2,384]{1,0:T(2,128)} fusion(pred[2,2304]{1,0:T(4,128)(4,1)S(1)} %bitcast.90, bf16[2,2304,128]{2,1,0:T(8,128)(2,1)S(1)} %bitcast.80, bf16[4,2,384,128]{3,2,1,0:T(8,128)(2,1)S(1)} %get-tuple-element.146, s32[]{:T(128)} %get-tuple-element.136), kind=kOutput, calls=%fused_computation.33.clone.1 | convolution fusion | flops 460065024 | bytes 1388548 | tf_op jit(solution)/shard_map/while/body/eval_jaxpr/while/body/eval_jaxpr/sub | solution.py:32
  81.4 1.7 gather_fusion
  83.2 4.5 %fusion.62 = bf16[4,2,384,128]{3,2,1,0:T(8,128)(2,1)} fusion(bf16[4,2,384,128]{3,2,1,0:T(8,128)(2,1)} %get-tuple-element.137, s32[]{:T(128)} %get-tuple-element.136, bf16[2,2304,128]{2,1,0:T(8,128)(2,1)} %bitcast.82, f32[2,384]{1,0:T(2,128)} %fusion.61, pred[2,2304]{1,0:T(4,128)(4,1)S(1)} %bitcast.91, bf16[2,2304,128]{2,1,0:T(8,128)(2,1)S(1)} %bitcast.81, ...), kind=kOutput, calls=%fused_computation.13.clone.1 | convolution fusion | flops 914918400 | bytes 2765824 | tf_op jit(solution)/shard_map/while/body/eval_jaxpr/while/body/eval_jaxpr/gqk,gkd->gqd/dot_general | solution.py:34
  90.0 3.0 %fusion.61 = f32[2,384]{1,0:T(2,128)} fusion(pred[2,2304]{1,0:T(4,128)(4,1)S(1)} %bitcast.90, bf16[2,2304,128]{2,1,0:T(8,128)(2,1)S(1)} %bitcast.80, bf16[4,2,384,128]{3,2,1,0:T(8,128)(2,1)S(1)} %get-tuple-element.146, s32[]{:T(128)} %get-tuple-element.136), kind=kOutput, calls=%fused_computation.33.clone.1 | convolution fusion | flops 460065024 | bytes 1388548 | tf_op jit(solution)/shard_map/while/body/eval_jaxpr/while/body/eval_jaxpr/sub | solution.py:32
  93.0 1.7 gather_fusion
  94.7 4.5 %fusion.62 = bf16[4,2,384,128]{3,2,1,0:T(8,128)(2,1)} fusion(bf16[4,2,384,128]{3,2,1,0:T(8,128)(2,1)} %get-tuple-element.137, s32[]{:T(128)} %get-tuple-element.136, bf16[2,2304,128]{2,1,0:T(8,128)(2,1)} %bitcast.82, f32[2,384]{1,0:T(2,128)} %fusion.61, pred[2,2304]{1,0:T(4,128)(4,1)S(1)} %bitcast.91, bf16[2,2304,128]{2,1,0:T(8,128)(2,1)S(1)} %bitcast.81, ...), kind=kOutput, calls=%fused_computation.13.clone.1 | convolution fusion | flops 914918400 | bytes 2765824 | tf_op jit(solution)/shard_map/while/body/eval_jaxpr/while/body/eval_jaxpr/gqk,gkd->gqd/dot_general | solution.py:34
  101.5 3.0 %fusion.61 = f32[2,384]{1,0:T(2,128)} fusion(pred[2,2304]{1,0:T(4,128)(4,1)S(1)} %bitcast.90, bf16[2,2304,128]{2,1,0:T(8,128)(2,1)S(1)} %bitcast.80, bf16[4,2,384,128]{3,2,1,0:T(8,128)(2,1)S(1)} %get-tuple-element.146, s32[]{:T(128)} %get-tuple-element.136), kind=kOutput, calls=%fused_computation.33.clone.1 | convolution fusion | flops 460065024 | bytes 1388548 | tf_op jit(solution)/shard_map/while/body/eval_jaxpr/while/body/eval_jaxpr/sub | solution.py:32
  106.2 4.5 %fusion.62 = bf16[4,2,384,128]{3,2,1,0:T(8,128)(2,1)} fusion(bf16[4,2,384,128]{3,2,1,0:T(8,128)(2,1)} %get-tuple-element.137, s32[]{:T(128)} %get-tuple-element.136, bf16[2,2304,128]{2,1,0:T(8,128)(2,1)} %bitcast.82, f32[2,384]{1,0:T(2,128)} %fusion.61, pred[2,2304]{1,0:T(4,128)(4,1)S(1)} %bitcast.91, bf16[2,2304,128]{2,1,0:T(8,128)(2,1)S(1)} %bitcast.81, ...), kind=kOutput, calls=%fused_computation.13.clone.1 | convolution fusion | flops 914918400 | bytes 2765824 | tf_op jit(solution)/shard_map/while/body/eval_jaxpr/while/body/eval_jaxpr/gqk,gkd->gqd/dot_general | solution.py:34
  111.2 2.4 %reduce = bf16[3072,128]{1,0:T(8,128)(2,1)S(1)} reduce(bf16[3072,1,1,128]{3,0,2,1:T(8,128)(2,1)} %bitcast.89, bf16[]{:T(256)} %broadcast.45), dimensions={1,2}, to_apply=%copy.33.reduce_sub_computation | reduce | bytes 1572866 | tf_op jit(solution)/shard_map/broadcast_in_dim;transpose | solution.py:68
  113.8 20.7 %all_to_all.60 = bf16[8,2,24576]{2,1,0:T(2,128)(2,1)S(1)} all-to-all(bf16[8,2,24576]{2,1,0:T(2,128)(2,1)S(1)} %reshape.96), channel_id=1, replica_groups=mesh['dp'=16,'ulysses'=8,'tensor'=2] {'ulysses'}, dimensions={0} | all-to-all | bytes 1572864 | tf_op jit(solution)/shard_map/all_to_all | solution.py:69
  135.8 7.6 %fusion.41 = f32[384,3072]{1,0:T(8,128)} fusion(bf16[384,1024]{0,1:T(8,128)(2,1)S(1)} %bitcast.83, bf16[1024,3072]{1,0:T(8,128)(2,1)} %all-gather.2.cloned.1.call-done), kind=kOutput, calls=%fused_computation.34 | convolution fusion | flops 2415919104 | bytes 11796480 | tf_op jit(solution)/shard_map/dot_general | solution.py:71
  143.5 63.7 %reduce-scatter.2.cloned.1.call-done = f32[384,1536]{1,0:T(8,128)} async-done(((f32[384,3072]{1,0:T(8,128)}), f32[384,1536]{1,0:T(8,128)}) %reduce-scatter.2.cloned.1.call-update) | async-done | bytes 2359312 | tf_op jit(solution)/shard_map/reduce_scatter | solution.py:76
  207.2 2.8 %convert_element_type.9 = bf16[384,1536]{1,0:T(8,128)(2,1)} convert(f32[384,1536]{1,0:T(8,128)} %reduce-scatter.2.cloned.1.call-done) | non-fusion elementwise | flops 589824 | bytes 3538944 | tf_op jit(solution)/shard_map/convert_element_type | solution.py:76
  (49 shorter events, 17.2 us)
Async XLA Ops:
  6.5 10.4 %copy-start = (bf16[384,1024]{1,0:T(8,128)(2,1)S(1)}, bf16[384,1024]{1,0:T(8,128)(2,1)}, u32[]{:S(2)}) copy-start(bf16[384,1024]{1,0:T(8,128)(2,1)} %param.9) | copy-start | bytes 2359300
  6.5 28.3 %copy-start.1 = (bf16[384,1024]{1,0:T(8,128)(2,1)S(1)}, bf16[384,1024]{1,0:T(8,128)(2,1)}, u32[]{:S(2)}) copy-start(bf16[384,1024]{1,0:T(8,128)(2,1)} %param.7) | copy-start | bytes 2359300
  6.5 129.3 %all-gather.2.cloned.1.call-start = ((), (), s32[]{:S(2)}) async-start(), calls=%async_computation.5 | async-start | bytes 7077888 | tf_op jit(solution)/shard_map/all_gather | solution.py:73
  9.5 19.2 %all-to-all-start.1 = ((bf16[384,8,1,128]{0,3,2,1:T(8,128)(2,1)}), bf16[384,8,1,128]{0,3,2,1:T(8,128)(2,1)S(1)}, u32[]{:S(2)}, u32[]{:S(2)}) async-start(bf16[384,8,1,128]{0,3,2,1:T(8,128)(2,1)} %bitcast.11), calls=%async_computation.1 | async-start | bytes 1572864 | tf_op jit(solution)/shard_map/all_to_all | solution.py:52
  28.8 17.8 %all-to-all-start.2 = ((bf16[384,8,1,128]{0,3,2,1:T(8,128)(2,1)}), bf16[384,8,1,128]{0,3,2,1:T(8,128)(2,1)S(1)}, u32[]{:S(2)}, u32[]{:S(2)}) async-start(bf16[384,8,1,128]{0,3,2,1:T(8,128)(2,1)} %bitcast.16), calls=%async_computation.2 | async-start | bytes 1572864 | tf_op jit(solution)/shard_map/all_to_all | solution.py:55
  46.6 18.0 %all-to-all-start = ((bf16[384,8,1,128]{3,0,2,1:T(8,128)(2,1)}), bf16[384,8,1,128]{3,0,2,1:T(8,128)(2,1)S(1)}, u32[]{:S(2)}, u32[]{:S(2)}) async-start(bf16[384,8,1,128]{3,0,2,1:T(8,128)(2,1)} %copy.26), calls=%async_computation | async-start | bytes 1572864 | tf_op jit(solution)/shard_map/all_to_all | solution.py:51
  55.0 152.2 %reduce-scatter.2.cloned.1.call-start = ((), (), s32[]{:S(2)}) async-start(), calls=%async_computation.6 | async-start | bytes 7077888 | tf_op jit(solution)/shard_map/reduce_scatter | solution.py:76
Sparse Core Ops, SparseCore 0:
  9.8 123.7 all-gather.1
  143.6 63.5 reduce-scatter.1
where the time goes:
time: 218 us; the launch traced here: 217 us
  waiting for transfers between devices  94.2 us (43%)
  matrix products  37.4 us (17%)
  starting transfers between devices  21.9 us (10%)
  blocking collectives  20.7 us (9%)
  local copies, waits for them, and re-layouts  18.5 us (8%)
  between operations  13.5 us (6%)
  other arithmetic  10.7 us (5%)
    reduce_scatter x1, waiting for transfers between devices, on_device(): lax.psum_scatter(partial_out, 'tensor', scatter_dimension=1, tiled=True)  63.7 us
    all_to_all x1, blocking collectives, on_device(): lax.all_to_all(attention, 'ulysses', split_axis=0, concat_axis=1, tiled=T...  20.7 us
    dot_general x4, matrix products, per_group(): jnp.einsum('gqk,gkd->gqd', weights, value_block, preferred_element_type=j...  17.9 us
    sub x4, matrix products, per_group(): exp_scores = jnp.exp(scores - peak_score)  11.9 us
    all_to_all x1, waiting for transfers between devices, on_device(): lax.all_to_all(arrange(key_vectors), 'ulysses', split_axis=1, concat_axis...  10.7 us
    all_to_all x1, waiting for transfers between devices, on_device(): lax.all_to_all(arrange(value_vectors), 'ulysses', split_axis=1, concat_ax...  10.2 us
    all_to_all x1, waiting for transfers between devices, on_device(): lax.all_to_all(arrange(queries), 'ulysses', split_axis=1, concat_axis=0,...  8.83 us
    all_to_all x1, starting transfers between devices, on_device(): lax.all_to_all(arrange(queries), 'ulysses', split_axis=1, concat_axis=0,...  8.43 us
  transfers between devices with their start and end apart: 5, of which 4 were waited for; matrix products, arithmetic and copies ran while one was open for 26% of the time, Pallas kernels for 0%

commit v1 on v0

v1 whole, which is shorter than its diff:
```python
import functools
import math

import jax
import jax.numpy as jnp
from jax import lax
from jax.experimental import pallas as pl
from jax.experimental.pallas import tpu as pltpu
from jax.sharding import PartitionSpec as P

HD = 128
TILE = 384
WMAX = 6
ROWS = 128
MESH = pl.DeviceIdType.MESH
COEF = HD ** (-0.5) * math.log2(math.e)
FAR = 1e30


def attend(tile, count, window, q_tile, k_tiles, v_tiles, scores, put):
    first = 2 * jnp.maximum(lax.div(tile, 2) - 1, 0)
    away = []
    for j in range(count):
        listed = window[tile, 0] == first + j
        for s in range(1, WMAX):
            listed = listed | (window[tile, s] == first + j)
        away.append(jnp.where(listed, 0.0, FAR).astype(jnp.float32))
    for block in range(TILE // ROWS):
        rows = pl.ds(block * ROWS, ROWS)
        held = scores.at[block % 2]
        q = q_tile[tile, rows, :]
        peak = None
        for j in range(count):
            s = lax.dot_general(
                q, k_tiles[first + j], (((1,), (1,)), ((), ())), preferred_element_type=jnp.float32
            )
            held[:, pl.ds(j * TILE, TILE)] = s
            top = jnp.maximum(jnp.maximum(s[:, :HD], s[:, HD : 2 * HD]), s[:, 2 * HD :]) - away[j]
            peak = top if peak is None else jnp.maximum(peak, top)
        peak = jnp.max(peak, axis=1, keepdims=True) * COEF
        total = None
        mixed = None
        for j in range(count):
            e = jnp.exp2(held[:, pl.ds(j * TILE, TILE)] * COEF - (peak + away[j]))
            part = e[:, :HD] + e[:, HD : 2 * HD] + e[:, 2 * HD :]
            total = part if total is None else total + part
            term = jnp.dot(
                e.astype(jnp.bfloat16), v_tiles[first + j], preferred_element_type=jnp.float32
            )
            mixed = term if mixed is None else mixed + term
        total = jnp.sum(total, axis=1, keepdims=True)
        put(rows, (mixed / total).astype(jnp.bfloat16))


def kernel(
    window, q_ref, k_ref, v_ref, w_ref, out_ref,
    qb, kb, vb, ob, done, wb, scores, acc,
    s_qkv, r_qkv, s_w, r_w, s_ring, r_ring, s_sib, r_sib, s_o, r_o,
):
    dp, u, t = lax.axis_index("dp"), lax.axis_index("ulysses"), lax.axis_index("tensor")
    z, c = lax.div(dp, 2), lax.rem(dp, 2)
    y, w = lax.div(u, 2), lax.rem(u, 2)

    def ahead(k):
        return lax.rem(y + lax.div(k, 2), 4) * 2 + lax.rem(w + lax.rem(k, 2), 2)

    def behind(k):
        return lax.rem(y + 4 - lax.div(k, 2), 4) * 2 + lax.rem(w + lax.rem(k, 2), 2)

    up = (lax.rem(z + 1, 8) * 2 + c, u, t)
    down = (lax.rem(z + 7, 8) * 2 + c, u, t)
    sibling = (z * 2 + 1 - c, u, t)

    barrier = pltpu.get_barrier_semaphore()
    for k in range(8):
        for other in range(2):
            if k or other:
                pl.semaphore_signal(
                    barrier, inc=1, device_id=(dp, ahead(k), lax.rem(t + other, 2)), device_id_type=MESH
                )
    for device in (up, down, sibling):
        pl.semaphore_signal(barrier, inc=1, device_id=device, device_id_type=MESH)
    pl.semaphore_wait(barrier, 18)

    def remote(src, dst, send, recv, device):
        return pltpu.make_async_remote_copy(
            src_ref=src, dst_ref=dst, send_sem=send, recv_sem=recv, device_id=device, device_id_type=MESH
        )

    def landed(ref, sem):
        pltpu.make_async_copy(ref, ref, sem).wait()

    side, place = lax.div(u, 4), lax.rem(u, 4)
    piece = w_ref.at[pl.ds(pl.multiple_of(z * 128 + c * 64, 64), 64), :]
    spot = wb.at[z, t, c, :, pl.ds(pl.multiple_of(place * 384, 384), 384)]
    own = side == t

    @pl.when(own)
    def _():
        pltpu.make_async_copy(piece, spot, r_w.at[t, place]).start()

    @pl.when(jnp.logical_not(own))
    def _():
        remote(piece, spot, s_w.at[0], r_w.at[t, place], (dp, u, side)).start()

    for k in range(1, 8):
        remote(piece, spot, s_w.at[k], r_w.at[t, place], (dp, ahead(k), side)).start()

    arrays = ((k_ref, kb), (v_ref, vb), (q_ref, qb))

    def cut(ref, i):
        return ref.at[:, pl.ds(pl.multiple_of(i * HD, HD), HD)]

    for a, (ref, buf) in enumerate(arrays):
        pltpu.make_async_copy(cut(ref, u), buf.at[u], r_qkv.at[a, u]).start()
        for k in range(1, 8):
            remote(
                cut(ref, ahead(k)), buf.at[u], s_qkv.at[a, k], r_qkv.at[a, u], (dp, ahead(k), t)
            ).start()

    def share(plane, half, slot):
        ref = wb.at[plane, half, c]
        remote(ref, ref, s_sib.at[slot, half], r_sib.at[plane, half], sibling).start()

    def pass_on(plane, half, way, distance):
        ref = wb.at[plane, half, c]
        remote(
            ref, ref, s_ring.at[way, distance - 1, half], r_ring.at[way, distance - 1, half],
            down if way else up,
        ).start()

    for half in range(2):
        for i in range(4):
            landed(wb.at[z, half, c, :, pl.ds(i * 384, 384)], r_w.at[half, i])
    for half in range(2):
        pass_on(z, half, 0, 1)
        pass_on(z, half, 1, 1)
    for half in range(2):
        share(z, half, 0)

    def ring(distance):
        for half in range(2):
            for way in range(2):
                if distance == 4 and half != way:
                    continue
                plane = lax.rem(z + (distance if way else 8 - distance), 8)
                landed(wb.at[plane, half, c], r_ring.at[way, distance - 1, half])
                if distance < 3 or (distance == 3 and half == way):
                    pass_on(plane, half, way, distance + 1)
                slot = 4 if distance == 4 else distance + 4 * way
                share(plane, half, slot)

    ring(1)
    for a in range(2):
        for i in range(8):
            landed(arrays[a][1].at[i], r_qkv.at[a, i])

    def step(k, carry):
        tile = ahead(k)
        landed(qb.at[tile], r_qkv.at[2, tile])

        def put(rows, value):
            done[k, rows, :] = value

        edge = (tile < 2) | (tile >= 6)

        @pl.when(edge)
        def _():
            attend(tile, 4, window, qb, kb, vb, scores, put)

        @pl.when(jnp.logical_not(edge))
        def _():
            attend(tile, 6, window, qb, kb, vb, scores, put)

        @pl.when(k == 0)
        def _():
            pltpu.make_async_copy(done.at[k], ob.at[u, t], r_o.at[u, t]).start()

        @pl.when(k > 0)
        def _():
            remote(done.at[k], ob.at[u, t], s_o.at[k, 0], r_o.at[u, t], (dp, tile, t)).start()

        remote(done.at[k], ob.at[u, t], s_o.at[k, 1], r_o.at[u, t], (dp, tile, 1 - t)).start()
        for distance, at in ((2, 0), (3, 3), (4, 6)):

            @pl.when(k == at)
            def _():
                ring(distance)

        return carry

    lax.fori_loop(0, 8, step, 0)

    for plane in range(8):
        for half in range(2):
            landed(wb.at[plane, half, 1 - c], r_sib.at[plane, half])

    def project(k, carry):
        source = behind(k)
        for half in range(2):
            landed(ob.at[source, half], r_o.at[source, half])
        rows = jnp.concatenate([ob[source, 0], ob[source, 1]], axis=1)
        for n in range(3):
            columns = pl.ds(n * 512, 512)
            term = jnp.dot(
                rows, wb[source, :, :, :, columns].reshape(256, 512), preferred_element_type=jnp.float32
            )

            @pl.when(k == 0)
            def _():
                acc[:, columns] = term

            @pl.when((k > 0) & (k < 7))
            def _():
                acc[:, columns] += term

            @pl.when(k == 7)
            def _():
                out_ref[:, columns] = (acc[:, columns] + term).astype(jnp.bfloat16)

        return carry

    lax.fori_loop(0, 8, project, 0)

    @pl.when(jnp.logical_not(own))
    def _():
        remote(piece, spot, s_w.at[0], r_w.at[t, place], (dp, u, side)).wait_send()

    for k in range(1, 8):
        remote(piece, spot, s_w.at[k], r_w.at[t, place], (dp, ahead(k), side)).wait_send()
    for a, (ref, buf) in enumerate(arrays):
        for k in range(1, 8):
            remote(
                cut(ref, ahead(k)), buf.at[u], s_qkv.at[a, k], r_qkv.at[a, u], (dp, ahead(k), t)
            ).wait_send()
    for half in range(2):
        for way in range(2):
            for distance in range(1, 5):
                if distance < 4 or half == way:
                    ref = wb.at[z, half, c]
                    remote(
                        ref, ref, s_ring.at[way, distance - 1, half], r_ring.at[way, distance - 1, half],
                        down if way else up,
                    ).wait_send()
        for slot in range(8):
            ref = wb.at[z, half, c]
            remote(ref, ref, s_sib.at[slot, half], r_sib.at[z, half], sibling).wait_send()
    for k in range(8):
        if k:
            remote(done.at[k], ob.at[u, t], s_o.at[k, 0], r_o.at[u, t], (dp, ahead(k), t)).wait_send()
        remote(done.at[k], ob.at[u, t], s_o.at[k, 1], r_o.at[u, t], (dp, ahead(k), 1 - t)).wait_send()


def on_device(queries, key_vectors, value_vectors, window_tiles, out_weight):
    dma = pltpu.SemaphoreType.DMA
    bf16, f32 = jnp.bfloat16, jnp.float32
    return pl.pallas_call(
        kernel,
        out_shape=jax.ShapeDtypeStruct((TILE, 1536), bf16),
        in_specs=[pl.BlockSpec(memory_space=pltpu.SMEM)] + [pl.BlockSpec(memory_space=pl.ANY)] * 4,
        out_specs=pl.BlockSpec(memory_space=pltpu.VMEM),
        scratch_shapes=[
            pltpu.VMEM((8, TILE, HD), bf16),
            pltpu.VMEM((8, TILE, HD), bf16),
            pltpu.VMEM((8, TILE, HD), bf16),
            pltpu.VMEM((8, 2, TILE, HD), bf16),
            pltpu.VMEM((8, TILE, HD), bf16),
            pltpu.VMEM((8, 2, 2, 64, 1536), bf16),
            pltpu.VMEM((2, ROWS, WMAX * TILE), f32),
            pltpu.VMEM((TILE, 1536), f32),
            dma((3, 8)), dma((3, 8)), dma((8,)), dma((2, 4)),
            dma((2, 4, 2)), dma((2, 4, 2)), dma((8, 2)), dma((8, 2)), dma((8, 2)), dma((8, 2)),
        ],
        compiler_params=pltpu.CompilerParams(
            collective_id=0, has_side_effects=True, vmem_limit_bytes=44 << 20
        ),
        name="tile_attention",
    )(window_tiles, queries, key_vectors, value_vectors, out_weight)


def solution(mesh):
    in_specs = (
        P(("dp", "ulysses"), "tensor"),
        P(("dp", "ulysses"), "tensor"),
        P(("dp", "ulysses"), "tensor"),
        P("dp", None),
        P("tensor", "ulysses"),
    )
    out_specs = P(("dp", "ulysses"), "tensor")
    return jax.shard_map(
        on_device, mesh=mesh, in_specs=in_specs, out_specs=out_specs, check_vma=False
    )
```

time: 218 us -> 103 us (0.47)
  Pallas kernels: 0 us -> 96.1 us
  waiting for transfers between devices: 94.2 us -> 0 us
  matrix products: 37.4 us -> 0 us
  starting transfers between devices: 21.9 us -> 0 us
  blocking collectives: 20.7 us -> 0 us
  between operations: 13.5 us -> 0.01 us
  local copies, waits for them, and re-layouts: 18.5 us -> 6.23 us
  other arithmetic: 10.7 us -> 0 us
    pallas_call x0 -> x1, Pallas kernels: none -> 96.1 us  [on_device(): pl.pallas_call(kernel, out_shape=jax.ShapeDtypeStruct((TILE, 1536), bf16)...]
    reduce_scatter x1 -> x0, waiting for transfers between devices: 63.7 us -> none  [on_device(): lax.psum_scatter(partial_out, 'tensor', scatter_dimension=1, tiled=True)]
    all_to_all x3 -> x0, waiting for transfers between devices: 29.7 us -> none  [the longest x1 10.7 us: on_device(): lax.all_to_all(arrange(key_vectors), 'ulysses', split_axis=1, concat_axis...]
    dot_general x5 -> x0, matrix products: 25.5 us -> none  [the longest x4 17.9 us: per_group(): jnp.einsum('gqk,gkd->gqd', weights, value_block, preferred_element_type=j...]
    all_to_all x3 -> x0, starting transfers between devices: 21.9 us -> none  [the longest x1 8.43 us: on_device(): lax.all_to_all(arrange(queries), 'ulysses', split_axis=1, concat_axis=0,...]
    all_to_all x1 -> x0, blocking collectives: 20.7 us -> none  [on_device(): lax.all_to_all(attention, 'ulysses', split_axis=0, concat_axis=1, tiled=T...]
    sub x4 -> x0, matrix products: 11.9 us -> none  [per_group(): exp_scores = jnp.exp(scores - peak_score)]
    gather x8 -> x0, local copies, waits for them, and re-layouts: 10.1 us -> none  [the longest x4 6.99 us: per_group(): value_block = value_tiles[safe_index].reshape(2, WMAX * TILE, HD)]
  transfers between devices with their start and end apart: 5 -> 0, of which waited for: 4 -> 0; matrix products, arithmetic and copies ran while one was open for 26% -> 0% of each run, Pallas kernels for 0% -> 0%
where the time goes in v1:
time: 103 us; the launch traced here: 102 us
  Pallas kernels  96.1 us (93%)
  local copies, waits for them, and re-layouts  6.23 us (6%)
    pallas_call x1, Pallas kernels, on_device(): pl.pallas_call(kernel, out_shape=jax.ShapeDtypeStruct((TILE, 1536), bf16)...  96.1 us
    unnamed x11, local copies, waits for them, and re-layouts  6.23 us

profile of v1, /device:TPU:8, one launch (start us, length us, event | category | flops | bytes accessed | tf_op | source)
XLA Modules:
  0.0 102.3 jit_solution(7598230656529102868)
XLA Ops:
  0.0 0.0 copy-start
  0.0 1.1 %copy-done = bf16[384,1024]{1,0:T(8,128)(2,1)S(1)} copy-done((bf16[384,1024]{1,0:T(8,128)(2,1)S(1)}, bf16[384,1024]{1,0:T(8,128)(2,1)}, u32[]{:S(2)}) %copy-start) | copy-done | bytes 786456
  1.1 0.0 copy-start.1
  1.1 1.1 %copy-done.1 = bf16[384,1024]{1,0:T(8,128)(2,1)S(1)} copy-done((bf16[384,1024]{1,0:T(8,128)(2,1)S(1)}, bf16[384,1024]{1,0:T(8,128)(2,1)}, u32[]{:S(2)}) %copy-start.1) | copy-done | bytes 786456
  2.3 0.0 copy-start.2
  2.3 1.1 %copy-done.2 = bf16[384,1024]{1,0:T(8,128)(2,1)S(1)} copy-done((bf16[384,1024]{1,0:T(8,128)(2,1)S(1)}, bf16[384,1024]{1,0:T(8,128)(2,1)}, u32[]{:S(2)}) %copy-start.2) | copy-done | bytes 786456
  3.4 0.0 copy-start.3
  3.4 1.1 %copy-done.3 = bf16[1024,384]{1,0:T(8,128)(2,1)S(1)} copy-done((bf16[1024,384]{1,0:T(8,128)(2,1)S(1)}, bf16[1024,384]{1,0:T(8,128)(2,1)}, u32[]{:S(2)}) %copy-start.3) | copy-done | bytes 786456
  4.5 0.0 copy-start.4
  4.5 0.7 copy-done.4
  5.2 96.1 %tile_attention.1 = bf16[384,1536]{1,0:T(8,128)(2,1)S(1)} custom-call(s32[8,6]{1,0:T(8,128)S(1)} %copy-done.4, bf16[384,1024]{1,0:T(8,128)(2,1)S(1)} %copy-done, bf16[384,1024]{1,0:T(8,128)(2,1)S(1)} %copy-done.1, bf16[384,1024]{1,0:T(8,128)(2,1)S(1)} %copy-done.2, bf16[1024,384]{1,0:T(8,128)(2,1)S(1)} %copy-done.3), custom_call_target="tpu_custom_call" | custom-call | tf_op jit(solution)/shard_map/tile_attention/pallas_call | solution.py:257
  101.3 1.0 copy.7
Async XLA Ops:
  0.0 1.1 %copy-start = (bf16[384,1024]{1,0:T(8,128)(2,1)S(1)}, bf16[384,1024]{1,0:T(8,128)(2,1)}, u32[]{:S(2)}) copy-start(bf16[384,1024]{1,0:T(8,128)(2,1)} %q_ref.1) | copy-start | bytes 2359300
  1.1 1.1 %copy-start.1 = (bf16[384,1024]{1,0:T(8,128)(2,1)S(1)}, bf16[384,1024]{1,0:T(8,128)(2,1)}, u32[]{:S(2)}) copy-start(bf16[384,1024]{1,0:T(8,128)(2,1)} %k_ref.1) | copy-start | bytes 2359300
  2.3 1.1 %copy-start.2 = (bf16[384,1024]{1,0:T(8,128)(2,1)S(1)}, bf16[384,1024]{1,0:T(8,128)(2,1)}, u32[]{:S(2)}) copy-start(bf16[384,1024]{1,0:T(8,128)(2,1)} %v_ref.1) | copy-start | bytes 2359300
  3.4 1.1 %copy-start.3 = (bf16[1024,384]{1,0:T(8,128)(2,1)S(1)}, bf16[1024,384]{1,0:T(8,128)(2,1)}, u32[]{:S(2)}) copy-start(bf16[1024,384]{1,0:T(8,128)(2,1)} %w_ref.1) | copy-start | bytes 2359300
  4.5 0.7 copy-start.4

commit v2 on v1

--- a/solution.py
+++ b/solution.py
@@ -11,7 +11,6 @@
 HD = 128
 TILE = 384
 WMAX = 6
-ROWS = 128
 MESH = pl.DeviceIdType.MESH
 COEF = HD ** (-0.5) * math.log2(math.e)
 FAR = 1e30
@@ -25,37 +24,34 @@
         for s in range(1, WMAX):
             listed = listed | (window[tile, s] == first + j)
         away.append(jnp.where(listed, 0.0, FAR).astype(jnp.float32))
-    for block in range(TILE // ROWS):
-        rows = pl.ds(block * ROWS, ROWS)
-        held = scores.at[block % 2]
-        q = q_tile[tile, rows, :]
-        peak = None
-        for j in range(count):
-            s = lax.dot_general(
-                q, k_tiles[first + j], (((1,), (1,)), ((), ())), preferred_element_type=jnp.float32
-            )
-            held[:, pl.ds(j * TILE, TILE)] = s
-            top = jnp.maximum(jnp.maximum(s[:, :HD], s[:, HD : 2 * HD]), s[:, 2 * HD :]) - away[j]
-            peak = top if peak is None else jnp.maximum(peak, top)
-        peak = jnp.max(peak, axis=1, keepdims=True) * COEF
-        total = None
-        mixed = None
-        for j in range(count):
-            e = jnp.exp2(held[:, pl.ds(j * TILE, TILE)] * COEF - (peak + away[j]))
-            part = e[:, :HD] + e[:, HD : 2 * HD] + e[:, 2 * HD :]
-            total = part if total is None else total + part
-            term = jnp.dot(
-                e.astype(jnp.bfloat16), v_tiles[first + j], preferred_element_type=jnp.float32
-            )
-            mixed = term if mixed is None else mixed + term
-        total = jnp.sum(total, axis=1, keepdims=True)
-        put(rows, (mixed / total).astype(jnp.bfloat16))
+    q = q_tile[tile]
+    peak = None
+    for j in range(count):
+        s = lax.dot_general(
+            q, k_tiles[first + j], (((1,), (1,)), ((), ())), preferred_element_type=jnp.float32
+        )
+        scores[:, pl.ds(j * TILE, TILE)] = s
+        top = jnp.maximum(jnp.maximum(s[:, :HD], s[:, HD : 2 * HD]), s[:, 2 * HD :]) - away[j]
+        peak = top if peak is None else jnp.maximum(peak, top)
+    peak = jnp.max(peak, axis=1, keepdims=True) * COEF
+    total = None
+    mixed = None
+    for j in range(count):
+        e = jnp.exp2(scores[:, pl.ds(j * TILE, TILE)] * COEF - (peak + away[j]))
+        part = e[:, :HD] + e[:, HD : 2 * HD] + e[:, 2 * HD :]
+        total = part if total is None else total + part
+        term = jnp.dot(
+            e.astype(jnp.bfloat16), v_tiles[first + j], preferred_element_type=jnp.float32
+        )
+        mixed = term if mixed is None else mixed + term
+    total = jnp.sum(total, axis=1, keepdims=True)
+    put((mixed / total).astype(jnp.bfloat16))
 
 
 def kernel(
     window, q_ref, k_ref, v_ref, w_ref, out_ref,
     qb, kb, vb, ob, done, wb, scores, acc,
-    s_qkv, r_qkv, s_w, r_w, s_ring, r_ring, s_sib, r_sib, s_o, r_o,
+    s_qkv, r_qkv, s_w, r_w, s_ring, r_ring, s_sib, r_sib, s_o, r_o, level, ready,
 ):
     dp, u, t = lax.axis_index("dp"), lax.axis_index("ulysses"), lax.axis_index("tensor")
     z, c = lax.div(dp, 2), lax.rem(dp, 2)
@@ -72,15 +68,28 @@
     sibling = (z * 2 + 1 - c, u, t)
 
     barrier = pltpu.get_barrier_semaphore()
+    odd = lax.rem(z, 2)
+
+    def tell(sem, device):
+        pl.semaphore_signal(sem, inc=1, device_id=device, device_id_type=MESH)
+
     for k in range(8):
         for other in range(2):
             if k or other:
-                pl.semaphore_signal(
-                    barrier, inc=1, device_id=(dp, ahead(k), lax.rem(t + other, 2)), device_id_type=MESH
-                )
-    for device in (up, down, sibling):
-        pl.semaphore_signal(barrier, inc=1, device_id=device, device_id_type=MESH)
-    pl.semaphore_wait(barrier, 18)
+                tell(barrier, (dp, ahead(k), lax.rem(t + other, 2)))
+    tell(barrier, sibling)
+
+    @pl.when(odd == 0)
+    def _():
+        tell(barrier, up)
+        tell(barrier, down)
+
+    pl.semaphore_wait(barrier, 16 + 2 * odd)
+
+    @pl.when(odd == 1)
+    def _():
+        tell(ready, up)
+        tell(ready, down)
 
     def remote(src, dst, send, recv, device):
         return pltpu.make_async_remote_copy(
@@ -106,17 +115,39 @@
     for k in range(1, 8):
         remote(piece, spot, s_w.at[k], r_w.at[t, place], (dp, ahead(k), side)).start()
 
+    for k in range(1, 8):
+        remote(piece, spot, s_w.at[k], r_w.at[t, place], (dp, ahead(k), side)).wait_send()
+
+    @pl.when(jnp.logical_not(own))
+    def _():
+        remote(piece, spot, s_w.at[0], r_w.at[t, place], (dp, u, side)).wait_send()
+
+    x = 2 * w + t
+    for step in (1, 3):
+        beside = lax.rem(x + step, 4)
+        tell(level, (dp, 2 * y + lax.div(beside, 2), lax.rem(beside, 2)))
+        tell(level, (dp, 2 * lax.rem(y + step, 4) + w, t))
+    pl.semaphore_wait(level, 4)
+
     arrays = ((k_ref, kb), (v_ref, vb), (q_ref, qb))
 
     def cut(ref, i):
         return ref.at[:, pl.ds(pl.multiple_of(i * HD, HD), HD)]
 
-    for a, (ref, buf) in enumerate(arrays):
+    def send(a):
+        ref, buf = arrays[a]
         pltpu.make_async_copy(cut(ref, u), buf.at[u], r_qkv.at[a, u]).start()
         for k in range(1, 8):
             remote(
-                cut(ref, ahead(k)), buf.at[u], s_qkv.at[a, k], r_qkv.at[a, u], (dp, ahead(k), t)
+                cut(ref, behind(k)), buf.at[u], s_qkv.at[a, k], r_qkv.at[a, u], (dp, behind(k), t)
             ).start()
+
+    def have(a):
+        for i in range(8):
+            landed(arrays[a][1].at[i], r_qkv.at[a, i])
+
+    for a in range(3):
+        send(a)
 
     def share(plane, half, slot):
         ref = wb.at[plane, half, c]
@@ -132,6 +163,11 @@
     for half in range(2):
         for i in range(4):
             landed(wb.at[z, half, c, :, pl.ds(i * 384, 384)], r_w.at[half, i])
+
+    @pl.when(odd == 0)
+    def _():
+        pl.semaphore_wait(ready, 2)
+
     for half in range(2):
         pass_on(z, half, 0, 1)
         pass_on(z, half, 1, 1)
@@ -151,16 +187,16 @@
                 share(plane, half, slot)
 
     ring(1)
-    for a in range(2):
-        for i in range(8):
-            landed(arrays[a][1].at[i], r_qkv.at[a, i])
+    have(0)
+    have(1)
+    ring(2)
 
     def step(k, carry):
         tile = ahead(k)
         landed(qb.at[tile], r_qkv.at[2, tile])
 
-        def put(rows, value):
-            done[k, rows, :] = value
+        def put(value):
+            done[k] = value
 
         edge = (tile < 2) | (tile >= 6)
 
@@ -181,7 +217,7 @@
             remote(done.at[k], ob.at[u, t], s_o.at[k, 0], r_o.at[u, t], (dp, tile, t)).start()
 
         remote(done.at[k], ob.at[u, t], s_o.at[k, 1], r_o.at[u, t], (dp, tile, 1 - t)).start()
-        for distance, at in ((2, 0), (3, 3), (4, 6)):
+        for distance, at in ((3, 3),):
 
             @pl.when(k == at)
             def _():
@@ -191,47 +227,40 @@
 
     lax.fori_loop(0, 8, step, 0)
 
+    ring(4)
     for plane in range(8):
         for half in range(2):
             landed(wb.at[plane, half, 1 - c], r_sib.at[plane, half])
 
-    def project(k, carry):
-        source = behind(k)
-        for half in range(2):
-            landed(ob.at[source, half], r_o.at[source, half])
-        rows = jnp.concatenate([ob[source, 0], ob[source, 1]], axis=1)
+    def product(k, columns):
+        first, second = behind(k), behind(k + 1)
+        rows = jnp.concatenate([ob[first, 0], ob[first, 1], ob[second, 0], ob[second, 1]], axis=1)
+        part = [wb[source, :, :, :, columns].reshape(256, 512) for source in (first, second)]
+        return jnp.dot(rows, jnp.concatenate(part, axis=0), preferred_element_type=jnp.float32)
+
+    def arrived(k):
+        for i in range(2):
+            for half in range(2):
+                landed(ob.at[behind(k + i), half], r_o.at[behind(k + i), half])
+
+    def project(g, carry):
+        arrived(2 * g)
         for n in range(3):
             columns = pl.ds(n * 512, 512)
-            term = jnp.dot(
-                rows, wb[source, :, :, :, columns].reshape(256, 512), preferred_element_type=jnp.float32
-            )
-
-            @pl.when(k == 0)
-            def _():
-                acc[:, columns] = term
-
-            @pl.when((k > 0) & (k < 7))
-            def _():
-                acc[:, columns] += term
-
-            @pl.when(k == 7)
-            def _():
-                out_ref[:, columns] = (acc[:, columns] + term).astype(jnp.bfloat16)
-
+            acc[:, columns] += product(2 * g, columns)
         return carry
 
-    lax.fori_loop(0, 8, project, 0)
-
-    @pl.when(jnp.logical_not(own))
-    def _():
-        remote(piece, spot, s_w.at[0], r_w.at[t, place], (dp, u, side)).wait_send()
-
-    for k in range(1, 8):
-        remote(piece, spot, s_w.at[k], r_w.at[t, place], (dp, ahead(k), side)).wait_send()
+    acc[...] = jnp.zeros_like(acc)
+    lax.fori_loop(0, 3, project, 0)
+    arrived(6)
+    for n in range(3):
+        columns = pl.ds(n * 512, 512)
+        out_ref[:, columns] = (acc[:, columns] + product(6, columns)).astype(jnp.bfloat16)
+
     for a, (ref, buf) in enumerate(arrays):
         for k in range(1, 8):
             remote(
-                cut(ref, ahead(k)), buf.at[u], s_qkv.at[a, k], r_qkv.at[a, u], (dp, ahead(k), t)
+                cut(ref, behind(k)), buf.at[u], s_qkv.at[a, k], r_qkv.at[a, u], (dp, behind(k), t)
             ).wait_send()
     for half in range(2):
         for way in range(2):
@@ -266,13 +295,14 @@
             pltpu.VMEM((8, 2, TILE, HD), bf16),
             pltpu.VMEM((8, TILE, HD), bf16),
             pltpu.VMEM((8, 2, 2, 64, 1536), bf16),
-            pltpu.VMEM((2, ROWS, WMAX * TILE), f32),
+            pltpu.VMEM((TILE, WMAX * TILE), f32),
             pltpu.VMEM((TILE, 1536), f32),
             dma((3, 8)), dma((3, 8)), dma((8,)), dma((2, 4)),
             dma((2, 4, 2)), dma((2, 4, 2)), dma((8, 2)), dma((8, 2)), dma((8, 2)), dma((8, 2)),
+            pltpu.SemaphoreType.REGULAR, pltpu.SemaphoreType.REGULAR,
         ],
         compiler_params=pltpu.CompilerParams(
-            collective_id=0, has_side_effects=True, vmem_limit_bytes=44 << 20
+            collective_id=0, has_side_effects=True, vmem_limit_bytes=60 << 20
         ),
         name="tile_attention",
     )(window_tiles, queries, key_vectors, value_vectors, out_weight)

time: 103 us -> 74.2 us (0.72)
  Pallas kernels: 96.1 us -> 71.7 us
  local copies, waits for them, and re-layouts: 6.23 us -> 2.36 us
    pallas_call x1, Pallas kernels: 96.1 us -> 71.7 us  [on_device(): pl.pallas_call(kernel, out_shape=jax.ShapeDtypeStruct((TILE, 1536), bf16)...]
    unnamed x11 -> x1, local copies, waits for them, and re-layouts: 6.23 us -> 2.36 us
where the time goes in v2:
time: 74.2 us; the launch traced here: 74 us
  Pallas kernels  71.7 us (97%)
  local copies, waits for them, and re-layouts  2.36 us (3%)
    pallas_call x1, Pallas kernels, on_device(): pl.pallas_call(kernel, out_shape=jax.ShapeDtypeStruct((TILE, 1536), bf16)...  71.7 us
    unnamed x1, local copies, waits for them, and re-layouts  2.36 us

profile of v2, /device:TPU:8, one launch (start us, length us, event | category | flops | bytes accessed | tf_op | source)
XLA Modules:
  0.0 74.0 jit_solution(12157295323776390887)
XLA Ops:
  0.0 71.7 %tile_attention.1 = bf16[384,1536]{1,0:T(8,128)(2,1)} custom-call(s32[8,6]{1,0:T(8,128)} %window.1, bf16[384,1024]{1,0:T(8,128)(2,1)} %q_ref.1, bf16[384,1024]{1,0:T(8,128)(2,1)} %k_ref.1, bf16[384,1024]{1,0:T(8,128)(2,1)} %v_ref.1, bf16[1024,384]{1,0:T(8,128)(2,1)} %w_ref.1), custom_call_target="tpu_custom_call" | custom-call | tf_op jit(solution)/shard_map/tile_attention/pallas_call | solution.py:286
  71.7 2.4 %copy.7 = bf16[384,1536]{1,0:T(8,128)(2,1)} copy(bf16[384,1536]{1,0:T(8,128)(2,1)} %tile_attention.1) | data formatting | bytes 2359296

commit v3 on v2

--- a/solution.py
+++ b/solution.py
@@ -51,7 +51,7 @@
 def kernel(
     window, q_ref, k_ref, v_ref, w_ref, out_ref,
     qb, kb, vb, ob, done, wb, scores, acc,
-    s_qkv, r_qkv, s_w, r_w, s_ring, r_ring, s_sib, r_sib, s_o, r_o, level, ready,
+    s_qkv, r_qkv, s_w, r_w, s_ring, r_ring, s_sib, r_sib, s_o, r_o, level, ready, result, s_out,
 ):
     dp, u, t = lax.axis_index("dp"), lax.axis_index("ulysses"), lax.axis_index("tensor")
     z, c = lax.div(dp, 2), lax.rem(dp, 2)
@@ -187,11 +187,13 @@
                 share(plane, half, slot)
 
     ring(1)
+    acc[...] = jnp.zeros_like(acc)
     have(0)
     have(1)
     ring(2)
 
-    def step(k, carry):
+    def step(i, carry):
+        k = lax.rem(i * 5, 8)
         tile = ahead(k)
         landed(qb.at[tile], r_qkv.at[2, tile])
 
@@ -219,7 +221,7 @@
         remote(done.at[k], ob.at[u, t], s_o.at[k, 1], r_o.at[u, t], (dp, tile, 1 - t)).start()
         for distance, at in ((3, 3),):
 
-            @pl.when(k == at)
+            @pl.when(i == at)
             def _():
                 ring(distance)
 
@@ -232,30 +234,39 @@
         for half in range(2):
             landed(wb.at[plane, half, 1 - c], r_sib.at[plane, half])
 
-    def product(k, columns):
-        first, second = behind(k), behind(k + 1)
-        rows = jnp.concatenate([ob[first, 0], ob[first, 1], ob[second, 0], ob[second, 1]], axis=1)
-        part = [wb[source, :, :, :, columns].reshape(256, 512) for source in (first, second)]
+    def product(ks, columns):
+        sources = [behind(lax.rem(k * 5, 8)) for k in ks]
+        rows = jnp.concatenate([ob[source, half] for source in sources for half in range(2)], axis=1)
+        part = [wb[source, :, :, :, columns].reshape(256, 512) for source in sources]
         return jnp.dot(rows, jnp.concatenate(part, axis=0), preferred_element_type=jnp.float32)
 
     def arrived(k):
-        for i in range(2):
-            for half in range(2):
-                landed(ob.at[behind(k + i), half], r_o.at[behind(k + i), half])
+        source = behind(lax.rem(k * 5, 8))
+        for half in range(2):
+            landed(ob.at[source, half], r_o.at[source, half])
 
     def project(g, carry):
         arrived(2 * g)
+        arrived(2 * g + 1)
         for n in range(3):
             columns = pl.ds(n * 512, 512)
-            acc[:, columns] += product(2 * g, columns)
+            acc[:, columns] += product((2 * g, 2 * g + 1), columns)
         return carry
 
-    acc[...] = jnp.zeros_like(acc)
     lax.fori_loop(0, 3, project, 0)
     arrived(6)
     for n in range(3):
         columns = pl.ds(n * 512, 512)
-        out_ref[:, columns] = (acc[:, columns] + product(6, columns)).astype(jnp.bfloat16)
+        acc[:, columns] += product((6,), columns)
+    arrived(7)
+    for n in range(3):
+        columns = pl.ds(n * 512, 512)
+        result[:, columns] = (acc[:, columns] + product((7,), columns)).astype(jnp.bfloat16)
+        pltpu.make_async_copy(result.at[:, columns], out_ref.at[:, columns], s_out.at[n]).start()
+
+    for n in range(3):
+        columns = pl.ds(n * 512, 512)
+        pltpu.make_async_copy(result.at[:, columns], out_ref.at[:, columns], s_out.at[n]).wait()
 
     for a, (ref, buf) in enumerate(arrays):
         for k in range(1, 8):
@@ -287,7 +298,7 @@
         kernel,
         out_shape=jax.ShapeDtypeStruct((TILE, 1536), bf16),
         in_specs=[pl.BlockSpec(memory_space=pltpu.SMEM)] + [pl.BlockSpec(memory_space=pl.ANY)] * 4,
-        out_specs=pl.BlockSpec(memory_space=pltpu.VMEM),
+        out_specs=pl.BlockSpec(memory_space=pl.ANY),
         scratch_shapes=[
             pltpu.VMEM((8, TILE, HD), bf16),
             pltpu.VMEM((8, TILE, HD), bf16),
@@ -300,6 +311,7 @@
             dma((3, 8)), dma((3, 8)), dma((8,)), dma((2, 4)),
             dma((2, 4, 2)), dma((2, 4, 2)), dma((8, 2)), dma((8, 2)), dma((8, 2)), dma((8, 2)),
             pltpu.SemaphoreType.REGULAR, pltpu.SemaphoreType.REGULAR,
+            pltpu.VMEM((TILE, 1536), bf16), dma((3,)),
         ],
         compiler_params=pltpu.CompilerParams(
             collective_id=0, has_side_effects=True, vmem_limit_bytes=60 << 20

time: 74.2 us -> 70.5 us (0.950)
  Pallas kernels: 71.7 us -> 67.6 us
    pallas_call x1, Pallas kernels: 71.7 us -> 67.6 us  [on_device(): pl.pallas_call(kernel, out_shape=jax.ShapeDtypeStruct((TILE, 1536), bf16)...]
where the time goes in v3:
time: 70.5 us; the launch traced here: 70 us
  Pallas kernels  67.6 us (96%)
  local copies, waits for them, and re-layouts  2.36 us (3%)
    pallas_call x1, Pallas kernels, on_device(): pl.pallas_call(kernel, out_shape=jax.ShapeDtypeStruct((TILE, 1536), bf16)...  67.6 us
    unnamed x1, local copies, waits for them, and re-layouts  2.36 us

profile of v3, /device:TPU:8, one launch (start us, length us, event | category | flops | bytes accessed | tf_op | source)
XLA Modules:
  0.0 70.0 jit_solution(12017542299075981081)
XLA Ops:
  0.0 67.6 %tile_attention.1 = bf16[384,1536]{1,0:T(8,128)(2,1)} custom-call(s32[8,6]{1,0:T(8,128)} %window.1, bf16[384,1024]{1,0:T(8,128)(2,1)} %q_ref.1, bf16[384,1024]{1,0:T(8,128)(2,1)} %k_ref.1, bf16[384,1024]{1,0:T(8,128)(2,1)} %v_ref.1, bf16[1024,384]{1,0:T(8,128)(2,1)} %w_ref.1), custom_call_target="tpu_custom_call" | custom-call | tf_op jit(solution)/shard_map/tile_attention/pallas_call | solution.py:297
  67.6 2.4 %copy.7 = bf16[384,1536]{1,0:T(8,128)(2,1)} copy(bf16[384,1536]{1,0:T(8,128)(2,1)} %tile_attention.1) | data formatting | bytes 2359296

commit v4 on v3

--- a/solution.py
+++ b/solution.py
@@ -14,6 +14,7 @@
 MESH = pl.DeviceIdType.MESH
 COEF = HD ** (-0.5) * math.log2(math.e)
 FAR = 1e30
+ORDER = (0, 5, 2, 7, 4, 1, 6, 3)
 
 
 def attend(tile, count, window, q_tile, k_tiles, v_tiles, scores, put):
@@ -136,7 +137,6 @@
 
     def send(a):
         ref, buf = arrays[a]
-        pltpu.make_async_copy(cut(ref, u), buf.at[u], r_qkv.at[a, u]).start()
         for k in range(1, 8):
             remote(
                 cut(ref, behind(k)), buf.at[u], s_qkv.at[a, k], r_qkv.at[a, u], (dp, behind(k), t)
@@ -148,6 +148,8 @@
 
     for a in range(3):
         send(a)
+    for ref, buf, sem in ((k_ref, kb, 0), (v_ref, vb, 1), (q_ref, qb, 2)):
+        pltpu.make_async_copy(cut(ref, u), buf.at[u], r_qkv.at[sem, u]).start()
 
     def share(plane, half, slot):
         ref = wb.at[plane, half, c]
@@ -192,8 +194,8 @@
     have(1)
     ring(2)
 
-    def step(i, carry):
-        k = lax.rem(i * 5, 8)
+    def step(i, orders):
+        k = lax.rem(orders, 8)
         tile = ahead(k)
         landed(qb.at[tile], r_qkv.at[2, tile])
 
@@ -225,44 +227,45 @@
             def _():
                 ring(distance)
 
-        return carry
-
-    lax.fori_loop(0, 8, step, 0)
+        return lax.div(orders, 8)
+
+    lax.fori_loop(0, 8, step, sum(k * 8**i for i, k in enumerate(ORDER)))
 
     ring(4)
     for plane in range(8):
         for half in range(2):
             landed(wb.at[plane, half, 1 - c], r_sib.at[plane, half])
 
-    def product(ks, columns):
-        sources = [behind(lax.rem(k * 5, 8)) for k in ks]
+    def product(sources, columns):
         rows = jnp.concatenate([ob[source, half] for source in sources for half in range(2)], axis=1)
         part = [wb[source, :, :, :, columns].reshape(256, 512) for source in sources]
         return jnp.dot(rows, jnp.concatenate(part, axis=0), preferred_element_type=jnp.float32)
 
-    def arrived(k):
-        source = behind(lax.rem(k * 5, 8))
+    def arrived(source):
         for half in range(2):
             landed(ob.at[source, half], r_o.at[source, half])
 
-    def project(g, carry):
-        arrived(2 * g)
-        arrived(2 * g + 1)
+    def project(g, orders):
+        sources = behind(lax.rem(orders, 8)), behind(lax.rem(lax.div(orders, 8), 8))
+        for source in sources:
+            arrived(source)
         for n in range(3):
             columns = pl.ds(n * 512, 512)
-            acc[:, columns] += product((2 * g, 2 * g + 1), columns)
-        return carry
-
-    lax.fori_loop(0, 3, project, 0)
-    arrived(6)
-    for n in range(3):
-        columns = pl.ds(n * 512, 512)
-        acc[:, columns] += product((6,), columns)
-    arrived(7)
-    for n in range(3):
-        columns = pl.ds(n * 512, 512)
-        result[:, columns] = (acc[:, columns] + product((7,), columns)).astype(jnp.bfloat16)
-        pltpu.make_async_copy(result.at[:, columns], out_ref.at[:, columns], s_out.at[n]).start()
+            acc[:, columns] += product(sources, columns)
+        return lax.div(orders, 64)
+
+    lax.fori_loop(0, 3, project, sum(k * 8**i for i, k in enumerate(ORDER)))
+    for place in (6, 7):
+        source = behind(ORDER[place])
+        arrived(source)
+        for n in range(3):
+            columns = pl.ds(n * 512, 512)
+            total = acc[:, columns] + product((source,), columns)
+            if place == 6:
+                acc[:, columns] = total
+            else:
+                result[:, columns] = total.astype(jnp.bfloat16)
+                pltpu.make_async_copy(result.at[:, columns], out_ref.at[:, columns], s_out.at[n]).start()
 
     for n in range(3):
         columns = pl.ds(n * 512, 512)
@@ -291,10 +294,23 @@
         remote(done.at[k], ob.at[u, t], s_o.at[k, 1], r_o.at[u, t], (dp, ahead(k), 1 - t)).wait_send()
 
 
+def hand_over(source, target, held, s_in, s_out):
+    parts = [pl.ds(i * 96, 96) for i in range(4)]
+    reads = [pltpu.make_async_copy(source.at[p], held.at[p], s_in.at[i]) for i, p in enumerate(parts)]
+    writes = [pltpu.make_async_copy(held.at[p], target.at[p], s_out.at[i]) for i, p in enumerate(parts)]
+    for read in reads:
+        read.start()
+    for read, write in zip(reads, writes):
+        read.wait()
+        write.start()
+    for write in writes:
+        write.wait()
+
+
 def on_device(queries, key_vectors, value_vectors, window_tiles, out_weight):
     dma = pltpu.SemaphoreType.DMA
     bf16, f32 = jnp.bfloat16, jnp.float32
-    return pl.pallas_call(
+    mixed = pl.pallas_call(
         kernel,
         out_shape=jax.ShapeDtypeStruct((TILE, 1536), bf16),
         in_specs=[pl.BlockSpec(memory_space=pltpu.SMEM)] + [pl.BlockSpec(memory_space=pl.ANY)] * 4,
@@ -318,6 +334,14 @@
         ),
         name="tile_attention",
     )(window_tiles, queries, key_vectors, value_vectors, out_weight)
+    return pl.pallas_call(
+        hand_over,
+        out_shape=jax.ShapeDtypeStruct((TILE, 1536), bf16),
+        in_specs=[pl.BlockSpec(memory_space=pl.ANY)],
+        out_specs=pl.BlockSpec(memory_space=pl.ANY),
+        scratch_shapes=[pltpu.VMEM((TILE, 1536), bf16), dma((4,)), dma((4,))],
+        name="hand_over",
+    )(mixed)
 
 
 def solution(mesh):

time: 70.5 us -> 70.1 us (level)
  local copies, waits for them, and re-layouts: 2.36 us -> 0 us
  Pallas kernels: 67.6 us -> 69.7 us
    unnamed x1 -> x0, local copies, waits for them, and re-layouts: 2.36 us -> none
    pallas_call x0 -> x1, Pallas kernels: none -> 2.04 us  [on_device(): pl.pallas_call(hand_over, out_shape=jax.ShapeDtypeStruct((TILE, 1536), bf...]
where the time goes in v4:
time: 70.1 us; the launch traced here: 69.7 us
  Pallas kernels  69.7 us (99%)
    pallas_call x1, Pallas kernels, on_device(): pl.pallas_call(kernel, out_shape=jax.ShapeDtypeStruct((TILE, 1536), bf16)...  67.6 us
    pallas_call x1, Pallas kernels, on_device(): pl.pallas_call(hand_over, out_shape=jax.ShapeDtypeStruct((TILE, 1536), bf...  2.04 us

profile of v4, /device:TPU:8, one launch (start us, length us, event | category | flops | bytes accessed | tf_op | source)
XLA Modules:
  0.0 69.7 jit_solution(7816265272596033109)
XLA Ops:
  0.0 67.6 %tile_attention.1.source = bf16[384,1536]{1,0:T(8,128)(2,1)} custom-call(s32[8,6]{1,0:T(8,128)} %window.1, bf16[384,1024]{1,0:T(8,128)(2,1)} %q_ref.1, bf16[384,1024]{1,0:T(8,128)(2,1)} %k_ref.1, bf16[384,1024]{1,0:T(8,128)(2,1)} %v_ref.1, bf16[1024,384]{1,0:T(8,128)(2,1)} %w_ref.1), custom_call_target="tpu_custom_call" | custom-call | tf_op jit(solution)/shard_map/tile_attention/pallas_call | solution.py:313
  67.7 2.0 %hand_over.1 = bf16[384,1536]{1,0:T(8,128)(2,1)} custom-call(bf16[384,1536]{1,0:T(8,128)(2,1)} %tile_attention.1.source), custom_call_target="tpu_custom_call" | custom-call | tf_op jit(solution)/shard_map/hand_over/pallas_call | solution.py:337

commit v5 on v4

--- a/solution.py
+++ b/solution.py
@@ -232,10 +232,6 @@
     lax.fori_loop(0, 8, step, sum(k * 8**i for i, k in enumerate(ORDER)))
 
     ring(4)
-    for plane in range(8):
-        for half in range(2):
-            landed(wb.at[plane, half, 1 - c], r_sib.at[plane, half])
-
     def product(sources, columns):
         rows = jnp.concatenate([ob[source, half] for source in sources for half in range(2)], axis=1)
         part = [wb[source, :, :, :, columns].reshape(256, 512) for source in sources]
@@ -243,6 +239,7 @@
 
     def arrived(source):
         for half in range(2):
+            landed(wb.at[source, half, 1 - c], r_sib.at[source, half])
             landed(ob.at[source, half], r_o.at[source, half])
 
     def project(g, orders):

time: 70.1 us -> 70.1 us (level)
  no operation moved by 1% of the time
where the time goes in v5:
time: 70.1 us; the launch traced here: 69.7 us
  Pallas kernels  69.7 us (99%)
    pallas_call x1, Pallas kernels, on_device(): pl.pallas_call(kernel, out_shape=jax.ShapeDtypeStruct((TILE, 1536), bf16)...  67.6 us
    pallas_call x1, Pallas kernels, on_device(): pl.pallas_call(hand_over, out_shape=jax.ShapeDtypeStruct((TILE, 1536), bf...  2.04 us

profile of v5, /device:TPU:8, one launch (start us, length us, event | category | flops | bytes accessed | tf_op | source)
XLA Modules:
  0.0 69.7 jit_solution(5827448924726009040)
XLA Ops:
  0.0 67.6 %tile_attention.1.source = bf16[384,1536]{1,0:T(8,128)(2,1)} custom-call(s32[8,6]{1,0:T(8,128)} %window.1, bf16[384,1024]{1,0:T(8,128)(2,1)} %q_ref.1, bf16[384,1024]{1,0:T(8,128)(2,1)} %k_ref.1, bf16[384,1024]{1,0:T(8,128)(2,1)} %v_ref.1, bf16[1024,384]{1,0:T(8,128)(2,1)} %w_ref.1), custom_call_target="tpu_custom_call" | custom-call | tf_op jit(solution)/shard_map/tile_attention/pallas_call | solution.py:310
  67.7 2.0 %hand_over.1 = bf16[384,1536]{1,0:T(8,128)(2,1)} custom-call(bf16[384,1536]{1,0:T(8,128)(2,1)} %tile_attention.1.source), custom_call_target="tpu_custom_call" | custom-call | tf_op jit(solution)/shard_map/hand_over/pallas_call | solution.py:334
